TPU v7x, 32 devices: a whole 2x2x4 slice. The times are simulated.
32 devices in a mesh: row: 2 (over core), mesh: 16 (over z, y, x).
Axes of the slice: x: 2, y: 2, z: 4, core: 2. Of those that a mesh axis runs over, the one named last changes fastest.
Arguments:
- state: float32 [2, 7, 5, 512, 256], P('row', None, None, 'mesh'), may hold values from -6 to 6
- inverse_blocks: float32 [2, 5, 5, 512, 256], P('row', None, None, 'mesh'), may hold values from -0.25 to 0.5
- flux_jacobian: float32 [2, 5, 5], P('row'), may hold values from -2.5 to 2.5
- harmonics: int32 [2, 3], replicated, may hold values from 1 to 17, as said below
- interface_delay: float32 [2], replicated, may hold values from 0 to 1
- inflow: float32 [7, 5, 512], P(None, None, 'mesh'), may hold values from -6 to 6
- pairing: int32 [2, 512], P('row', 'mesh'), may hold values from 0 to 511, as said below
Outputs:
- updated: float32 [2, 7, 5, 512, 256], P('row', None, None, 'mesh')
Inputs may be any that keep to these rules, and one draw needn't show every extreme that they name: `harmonics`: each row's harmonic numbers leave the remainders 1 to 3 in some order when divided by 7. `pairing`: within each aligned block of 32 lines, a permutation of that block's lines.
All inputs are finite; a program needn't handle non-finite values.
Results may differ from a plain program's by a relative error of at most 0.00016.
Values sent between devices are 32-bit elements; how exact they have to be, the bound alone decides.
A program may use at most 64 MiB of HBM per device.

v0:
```python
import jax
import jax.numpy as jnp
from jax import lax
from jax.sharding import PartitionSpec as P

TIME_SAMPLES = 7
SECTIONS = 3


largest_mode = lax.Precision.HIGHEST
nu_second = 0.25
nu_fourth = 0.03
time_scale = 0.05


def from_behind(array, axis, by):
    devices = lax.axis_size(axis)
    pairs = [(i, i + by) for i in range(devices) if 0 <= i + by < devices]
    return lax.ppermute(array, axis, pairs)


def padded_2(array, sides, width):
    for axis, dim in sides:
        devices, length = (lax.axis_size(axis), array.shape[dim])
        up = [(i, (i + 1) % devices) for i in range(devices - 1)]
        down = [(j, i) for i, j in up]
        last = lax.slice_in_dim(array, length - width, length, axis=dim)
        first = lax.slice_in_dim(array, 0, width, axis=dim)
        before = lax.ppermute(last, axis, up)
        after = lax.ppermute(first, axis, down)
        array = jnp.concatenate([before, array, after], axis=dim)
    return array


def spectral_basis(sample_times, harmonic_modes):
    phase_angles = (
        2.0 * jnp.pi * sample_times[:, None] * harmonic_modes[None, :].astype(jnp.float32)
    )
    column_of_ones = jnp.ones((sample_times.shape[0], 1), jnp.float32)
    return jnp.concatenate([column_of_ones, jnp.cos(phase_angles), jnp.sin(phase_angles)], axis=1)


def basis_derivative(sample_times, harmonic_modes):
    angular_speeds = 2.0 * jnp.pi * harmonic_modes.astype(jnp.float32)
    phase_angles = sample_times[:, None] * angular_speeds[None, :]
    column_of_zeros = jnp.zeros((sample_times.shape[0], 1), jnp.float32)
    return jnp.concatenate(
        [
            column_of_zeros,
            -angular_speeds[None, :] * jnp.sin(phase_angles),
            angular_speeds[None, :] * jnp.cos(phase_angles),
        ],
        axis=1,
    )


def forward_transform(sample_times, harmonic_modes):
    sample_count = sample_times.shape[0]
    mode_weights = jnp.concatenate(
        [
            jnp.full((1,), 1.0 / sample_count, jnp.float32),
            jnp.full((sample_count - 1,), 2.0 / sample_count, jnp.float32),
        ]
    )
    return mode_weights[:, None] * spectral_basis(sample_times, harmonic_modes).T


def row_operators(harmonics, interface_delay, blade_row_index):
    sample_times = jnp.arange(TIME_SAMPLES, dtype=jnp.float32) / TIME_SAMPLES
    local_modes = harmonics[blade_row_index]
    upstream_modes = harmonics[jnp.maximum(blade_row_index - 1, 0)]
    spectral_derivative = jnp.dot(
        basis_derivative(sample_times, local_modes),
        forward_transform(sample_times, local_modes),
        precision=largest_mode,
        preferred_element_type=jnp.float32,
    )
    interface_mapping = jnp.dot(
        spectral_basis(sample_times + interface_delay[blade_row_index], upstream_modes),
        forward_transform(sample_times, upstream_modes),
        precision=largest_mode,
        preferred_element_type=jnp.float32,
    )
    return (spectral_derivative, interface_mapping)


def section_residual(padded, ghost_cells, spectral_derivative, flux_jac):
    centre = padded[:, :, 2:-2]
    before = jnp.concatenate([ghost_cells[:, :, :, None], centre[:, :, :, :-1]], axis=3)
    advection = jnp.einsum("ab,tbwl->tawl", flux_jac, centre - before, precision=largest_mode)
    second_diff = padded[:, :, 3:-1] - 2.0 * centre + padded[:, :, 1:-3]
    fourth_diff = (
        padded[:, :, 4:]
        - 4.0 * padded[:, :, 3:-1]
        + 6.0 * centre
        - 4.0 * padded[:, :, 1:-3]
        + padded[:, :, :-4]
    )
    temporal = jnp.einsum("ts,svwl->tvwl", spectral_derivative, centre, precision=largest_mode)
    return advection - nu_second * second_diff + nu_fourth * fourth_diff + time_scale * temporal


def apply_block(inverse, residual):
    total = inverse[None, :, 0] * residual[:, 0][:, None]
    for column_index in range(1, inverse.shape[1]):
        total = total + inverse[None, :, column_index] * residual[:, column_index][:, None]
    return total


def body(state, inverse_blocks, flux_jacobian, harmonics, interface_delay, inflow, pairing):
    blade_row_index = lax.axis_index("row")
    spectral_derivative, interface_mapping = row_operators(
        harmonics, interface_delay, blade_row_index
    )
    local_state = state[0]
    local_inverse = inverse_blocks[0]
    flux_jac = flux_jacobian[0]
    sample_count, variable_count, line_count, cell_count = local_state.shape
    outlet = local_state[:, :, :, -1]
    received = from_behind(outlet, "row", 1)
    upstream = jnp.where(blade_row_index == 0, inflow, received)
    local_pairs = pairing[0] - lax.axis_index("mesh") * line_count
    paired = jnp.take(upstream, local_pairs, axis=2)
    ghost_cells = jnp.einsum("ts,svw->tvw", interface_mapping, paired, precision=largest_mode)
    current = local_state
    for section_index in range(SECTIONS):
        padded = padded_2(current, (("mesh", 2),), 2)
        residual = section_residual(padded, ghost_cells, spectral_derivative, flux_jac)
        section_weight = (section_index + 1.0) / SECTIONS
        current = local_state - section_weight * apply_block(local_inverse, residual)
    return current[None]


def solution(mesh):
    return jax.shard_map(
        body,
        mesh=mesh,
        in_specs=(
            P("row", None, None, "mesh", None),
            P("row", None, None, "mesh", None),
            P("row", None, None),
            P(),
            P(),
            P(None, None, "mesh"),
            P("row", "mesh"),
        ),
        out_specs=P("row", None, None, "mesh", None),
        check_vma=False,
    )
```

profile of v0, /device:TPU:24, one launch (start us, length us, event | category | flops | bytes accessed | tf_op | source)
XLA Modules:
  0.0 86.9 jit_solution(15298913453960320041)
XLA Ops:
  0.0 1.9 %copy.150 = f32[1,7,5,32,256]{4,2,3,1,0:T(8,128)S(1)} copy(f32[1,7,5,32,256]{4,3,2,1,0:T(8,128)} %param.7) | data formatting | bytes 2293760 | tf_op args[0]
  1.9 0.7 fusion.136
  2.7 4.2 %collective-permute-start.1 = (f32[7,5,2,256]{3,1,2,0:T(8,128)}, f32[7,5,2,256]{3,1,2,0:T(8,128)}, u32[]{:S(2)}, u32[]{:S(2)}) collective-permute-start(f32[7,5,2,256]{3,1,2,0:T(8,128)} %get-tuple-element.24), channel_id=1, source_target_pairs={{1,0},{2,1},{3,2},{4,3},{5,4},{6,5},{7,6},{8,7},{9,8},{10,9},{11,1... | collective-permute-start | bytes 215048 | tf_op jit(solution)/shard_map/ppermute | solution.py:30
  6.9 1.9 %collective-permute-start.2 = (f32[7,5,2,256]{3,1,2,0:T(8,128)}, f32[7,5,2,256]{3,1,2,0:T(8,128)}, u32[]{:S(2)}, u32[]{:S(2)}) collective-permute-start(f32[7,5,2,256]{3,1,2,0:T(8,128)} %get-tuple-element.25), channel_id=1, source_target_pairs={{0,1},{1,2},{2,3},{3,4},{4,5},{5,6},{6,7},{7,8},{8,9},{9,10},{10,1... | collective-permute-start | bytes 215048 | tf_op jit(solution)/shard_map/ppermute | solution.py:29
  8.8 0.3 slice.199
  9.1 2.3 %copy.66 = f32[7,5,32,1]{1,0,2,3:T(8,128)} copy(f32[7,5,32,1]{3,1,2,0:T(8,128)S(1)} %slice.199) | data formatting | bytes 8960 | tf_op jit(solution)/shard_map/squeeze | solution.py:119
  11.4 2.1 %collective-permute-start = (f32[7,5,32]{1,0,2:T(8,128)}, f32[7,5,32]{1,0,2:T(8,128)}, u32[]{:S(2)}, u32[]{:S(2)}) collective-permute-start(f32[7,5,32]{1,0,2:T(8,128)} %bitcast.8), channel_id=1, source_target_pairs={{0,16},{1,17},{2,18},{3,19},{4,20},{5,21},{6,22},{7,23},{8,24},{9,... | collective-permute-start | bytes 13448 | tf_op jit(solution)/shard_map/ppermute | solution.py:19
  13.5 0.5 compare_and_fusion
  14.1 1.4 %slice_bitcast_fusion.2 = f32[1,7,5,32,255]{4,2,3,1,0:T(8,128)} fusion(f32[7,5,32,256]{3,1,2,0:T(8,128)S(1)} %bitcast.143), kind=kLoop, calls=%fused_computation.64 | loop fusion | bytes 2284800 | tf_op jit(solution)/shard_map/concatenate | solution.py:89
  15.5 0.6 dynamic_slice.9
  16.1 0.7 iota_multiply_fusion
  16.8 2.1 %slice_bitcast_fusion.7 = (f32[5,32,256]{2,1,0:T(8,128)S(1)}, f32[5,32,256]{2,1,0:T(8,128)}, f32[5,32,256]{2,1,0:T(8,128)}, f32[5,32,256]{2,1,0:T(8,128)}, f32[5,32,256]{2,1,0:T(8,128)}) fusion(f32[5,5,32,256]{3,2,1,0:T(8,128)} %bitcast.170), kind=kLoop, calls=%fused_computation.146 | loop fusion | bytes 1638400 | tf_op jit(solution)/shard_map/mul | solution.py:104
  18.9 0.1 fusion.95
  19.0 0.1 multiply_cosine_fusion.2
  19.2 0.2 convolution_bitcast_fusion.1
  19.4 2.9 %fusion.63 = f32[7,5,32,256]{3,0,2,1:T(8,128)} fusion(f32[7,7,1,1]{1,0,3,2:T(8,128)S(1)} %convolution_bitcast_fusion.1, f32[7,5,32,256]{3,2,1,0:T(8,128)S(1)} %bitcast.140), kind=kOutput, calls=%fused_computation.96 | convolution fusion | flops 24084480 | bytes 2293956 | tf_op jit(solution)/shard_map/ts,svwl->tvwl/dot_general | solution.py:99
  22.3 0.2 convolution_bitcast_fusion.2
  22.5 0.8 copy.39
  23.4 1.0 %copy.48 = f32[5,32,256]{2,0,1:T(8,128)S(1)} copy(f32[5,32,256]{2,1,0:T(8,128)} %get-tuple-element.27) | data formatting | bytes 327680 | tf_op jit(solution)/shard_map/mul | solution.py:106
  24.4 1.7 %copy.47 = f32[5,32,256]{2,0,1:T(8,128)} copy(f32[5,32,256]{2,1,0:T(8,128)} %get-tuple-element.28) | data formatting | bytes 327680 | tf_op jit(solution)/shard_map/mul | solution.py:106
  26.1 1.7 %copy.46 = f32[5,32,256]{2,0,1:T(8,128)} copy(f32[5,32,256]{2,1,0:T(8,128)} %get-tuple-element.29) | data formatting | bytes 327680 | tf_op jit(solution)/shard_map/mul | solution.py:106
  27.8 1.7 %copy.45 = f32[5,32,256]{2,0,1:T(8,128)} copy(f32[5,32,256]{2,1,0:T(8,128)} %get-tuple-element.30) | data formatting | bytes 327680 | tf_op jit(solution)/shard_map/mul | solution.py:106
  29.6 0.7 broadcast_select_fusion
  30.2 2.1 %gather_fusion = f32[32,7,5]{2,1,0:T(8,128)} fusion(f32[7,5,32]{1,0,2:T(8,128)} %broadcast_select_fusion, s32[1024]{0:T(1024)S(1)} %pad_clamp_fusion), kind=kCustom, calls=%fused_computation | custom fusion | bytes 9088 | tf_op jit(solution)/shard_map/jit(_take)/gather | solution.py:123
  32.4 1.7 %select_bitcast_fusion = f32[7,5,32]{1,0,2:T(8,128)} fusion(f32[32,7,5]{2,1,0:T(8,128)} %gather_fusion, pred[32]{0:T(512)(128)(4,1)S(1)} %copy-done.9), kind=kLoop, calls=%fused_computation.147 | loop fusion | flops 1120 | bytes 8992 | tf_op jit(solution)/shard_map/jit(_take)/select_n | solution.py:123
  34.0 1.0 %copy.40 = f32[7,5,32]{2,0,1:T(8,128)S(1)} copy(f32[7,5,32]{1,0,2:T(8,128)} %select_bitcast_fusion) | data formatting | bytes 8960 | tf_op jit(solution)/shard_map/jit(_take)/select_n | solution.py:123
  35.0 0.2 convolution_bitcast_fusion
  35.2 1.3 %copy.41 = f32[1,7,5,32,1]{4,2,3,1,0:T(8,128)} copy(f32[1,7,5,32,1]{3,1,2,4,0:T(8,128)S(1)} %convolution_bitcast_fusion) | data formatting | bytes 8960 | tf_op jit(solution)/shard_map/concatenate | solution.py:89
  36.5 5.9 %fusion.34 = f32[7,5,32,256]{3,1,2,0:T(8,128)S(1)} fusion(f32[7,5,32,256]{3,1,2,0:T(8,128)S(1)} %bitcast.144, f32[7,5,2,256]{3,1,2,0:T(8,128)} %collective-permute-done.2, f32[7,5,2,256]{3,1,2,0:T(8,128)} %collective-permute-done.1, f32[7,5,32,256]{3,0,2,1:T(8,128)} %fusion.63, f32[1,7,5,32,1]{4,2,3,1,0:T(8,128)} %copy.41, ...), kind=kOutput, calls=%fused_computation.59 | convolution fusion | flops 23511040 | bytes 5877860 | tf_op jit(solution)/shard_map/ab,tbwl->tawl/dot_general | solution.py:90
  42.5 1.0 %fusion.135 = (f32[7,1,32,256]{3,1,2,0:T(1,128)S(1)}, f32[7,1,32,256]{3,1,2,0:T(1,128)S(1)}, f32[7,1,32,256]{3,1,2,0:T(1,128)S(1)}, f32[7,1,32,256]{3,1,2,0:T(1,128)S(1)}, f32[7,1,32,256]{3,1,2,0:T(1,128)S(1)}) fusion(f32[7,5,32,256]{3,1,2,0:T(8,128)S(1)} %fusion.34), kind=kLoop, calls=%fused_computation.211 | loop fusion | bytes 2293760 | tf_op jit(solution)/shard_map/slice | solution.py:104
  43.7 1.6 %multiply_subtract_fusion.1 = f32[7,5,32,256]{3,1,2,0:T(8,128)S(1)} fusion(f32[7,32,256]{2,1,0:T(8,128)S(1)} %bitcast.153, f32[5,32,256]{2,0,1:T(8,128)S(1)} %copy.48, f32[7,32,256]{2,1,0:T(8,128)S(1)} %bitcast.157, f32[5,32,256]{2,0,1:T(8,128)S(1)} %copy-done.1, f32[7,32,256]{2,1,0:T(8,128)S(1)} %bitcast.159, f32[5,32,256]{2,0,1:T(8,128)S(1)} %copy-done.2, ...), kind=kLoop, calls=%fused_computation.85 | loop fusion | flops 3153920 | bytes 4259840 | tf_op jit(solution)/shard_map/sub | solution.py:130
  45.4 0.2 slice_bitcast_fusion.1
  45.6 5.7 %collective-permute-start.3 = (f32[7,5,2,256]{3,1,2,0:T(8,128)S(1)}, f32[7,5,2,256]{3,1,2,0:T(8,128)S(1)}, u32[]{:S(2)}, u32[]{:S(2)}) collective-permute-start(f32[7,5,2,256]{3,1,2,0:T(8,128)S(1)} %get-tuple-element.17), channel_id=1, source_target_pairs={{1,0},{2,1},{3,2},{4,3},{5,4},{6,5},{7,6},{8,7},{9,8},{10,9},{11,1... | collective-permute-start | bytes 215048 | tf_op jit(solution)/shard_map/ppermute | solution.py:30
  51.3 2.1 %collective-permute-start.4 = (f32[7,5,2,256]{3,1,2,0:T(8,128)S(1)}, f32[7,5,2,256]{3,1,2,0:T(8,128)S(1)}, u32[]{:S(2)}, u32[]{:S(2)}) collective-permute-start(f32[7,5,2,256]{3,1,2,0:T(8,128)S(1)} %get-tuple-element.18), channel_id=1, source_target_pairs={{0,1},{1,2},{2,3},{3,4},{4,5},{5,6},{6,7},{7,8},{8,9},{9,10},{10,1... | collective-permute-start | bytes 215048 | tf_op jit(solution)/shard_map/ppermute | solution.py:29
  53.4 1.8 %fusion.67 = f32[7,5,32,256]{3,0,2,1:T(8,128)S(1)} fusion(f32[7,7,1,1]{1,0,3,2:T(8,128)S(1)} %convolution_bitcast_fusion.1, f32[7,5,32,256]{3,1,2,0:T(8,128)S(1)} %multiply_subtract_fusion.1), kind=kOutput, calls=%fused_computation.100 | convolution fusion | flops 24084480 | bytes 2293956 | tf_op jit(solution)/shard_map/ts,svwl->tvwl/dot_general | solution.py:99
  55.2 4.5 %collective-permute-done.4 = f32[7,5,2,256]{3,1,2,0:T(8,128)S(1)} collective-permute-done((f32[7,5,2,256]{3,1,2,0:T(8,128)S(1)}, f32[7,5,2,256]{3,1,2,0:T(8,128)S(1)}, u32[]{:S(2)}, u32[]{:S(2)}) %collective-permute-start.4) | collective-permute-done | bytes 71712 | tf_op jit(solution)/shard_map/ppermute | solution.py:29
  59.8 4.8 %fusion.27 = f32[7,5,32,256]{3,1,2,0:T(8,128)S(1)} fusion(f32[7,5,32,256]{3,1,2,0:T(8,128)S(1)} %multiply_subtract_fusion.1, f32[7,5,2,256]{3,1,2,0:T(8,128)S(1)} %collective-permute-done.4, f32[7,5,2,256]{3,1,2,0:T(8,128)S(1)} %collective-permute-done.3, f32[7,5,32,256]{3,0,2,1:T(8,128)S(1)} %fusion.67, f32[1,7,5,32,1]{4,2,3,1,0:T(8,128)S(1)} %copy-done.4, ...), kind=kOutput, calls=%fused_computation.49 | convolution fusion | flops 26664960 | bytes 7843940 | tf_op jit(solution)/shard_map/ab,tbwl->tawl/dot_general | solution.py:90
  64.5 1.0 %fusion.133 = (f32[7,1,32,256]{3,1,2,0:T(1,128)S(1)}, f32[7,1,32,256]{3,1,2,0:T(1,128)S(1)}, f32[7,1,32,256]{3,1,2,0:T(1,128)S(1)}, f32[7,1,32,256]{3,1,2,0:T(1,128)S(1)}, f32[7,1,32,256]{3,1,2,0:T(1,128)S(1)}) fusion(f32[7,5,32,256]{3,1,2,0:T(8,128)S(1)} %fusion.27), kind=kLoop, calls=%fused_computation.209 | loop fusion | bytes 2293760 | tf_op jit(solution)/shard_map/slice | solution.py:104
  65.7 1.6 %multiply_subtract_fusion = f32[7,5,32,256]{3,1,2,0:T(8,128)S(1)} fusion(f32[7,32,256]{2,1,0:T(8,128)S(1)} %bitcast.147, f32[7,32,256]{2,1,0:T(8,128)S(1)} %bitcast.151, f32[7,32,256]{2,1,0:T(8,128)S(1)} %bitcast.155, f32[7,32,256]{2,1,0:T(8,128)S(1)} %bitcast.161, f32[7,32,256]{2,1,0:T(8,128)S(1)} %bitcast.145, f32[5,32,256]{2,0,1:T(8,128)S(1)} %copy.48, ...), kind=kLoop, calls=%fused_computation.74 | loop fusion | flops 3153920 | bytes 4259840 | tf_op jit(solution)/shard_map/sub | solution.py:130
  67.4 0.2 slice_bitcast_fusion
  67.6 1.9 %collective-permute-start.5 = (f32[7,5,2,256]{3,1,2,0:T(8,128)S(1)}, f32[7,5,2,256]{3,1,2,0:T(8,128)S(1)}, u32[]{:S(2)}, u32[]{:S(2)}) collective-permute-start(f32[7,5,2,256]{3,1,2,0:T(8,128)S(1)} %get-tuple-element.10), channel_id=1, source_target_pairs={{1,0},{2,1},{3,2},{4,3},{5,4},{6,5},{7,6},{8,7},{9,8},{10,9},{11,1... | collective-permute-start | bytes 215048 | tf_op jit(solution)/shard_map/ppermute | solution.py:30
  69.5 4.1 %collective-permute-start.6 = (f32[7,5,2,256]{3,1,2,0:T(8,128)S(1)}, f32[7,5,2,256]{3,1,2,0:T(8,128)S(1)}, u32[]{:S(2)}, u32[]{:S(2)}) collective-permute-start(f32[7,5,2,256]{3,1,2,0:T(8,128)S(1)} %get-tuple-element.11), channel_id=1, source_target_pairs={{0,1},{1,2},{2,3},{3,4},{4,5},{5,6},{6,7},{7,8},{8,9},{9,10},{10,1... | collective-permute-start | bytes 215048 | tf_op jit(solution)/shard_map/ppermute | solution.py:29
  73.6 1.8 %fusion.65 = f32[7,5,32,256]{3,0,2,1:T(8,128)S(1)} fusion(f32[7,7,1,1]{1,0,3,2:T(8,128)S(1)} %convolution_bitcast_fusion.1, f32[7,5,32,256]{3,1,2,0:T(8,128)S(1)} %multiply_subtract_fusion), kind=kOutput, calls=%fused_computation.98 | convolution fusion | flops 24084480 | bytes 2293956 | tf_op jit(solution)/shard_map/ts,svwl->tvwl/dot_general | solution.py:99
  75.5 2.5 %collective-permute-done.6 = f32[7,5,2,256]{3,1,2,0:T(8,128)S(1)} collective-permute-done((f32[7,5,2,256]{3,1,2,0:T(8,128)S(1)}, f32[7,5,2,256]{3,1,2,0:T(8,128)S(1)}, u32[]{:S(2)}, u32[]{:S(2)}) %collective-permute-start.6) | collective-permute-done | bytes 71712 | tf_op jit(solution)/shard_map/ppermute | solution.py:29
  78.0 4.8 %fusion.20 = f32[7,5,32,256]{3,1,2,0:T(8,128)S(1)} fusion(f32[7,5,32,256]{3,1,2,0:T(8,128)S(1)} %multiply_subtract_fusion, f32[7,5,2,256]{3,1,2,0:T(8,128)S(1)} %collective-permute-done.6, f32[7,5,2,256]{3,1,2,0:T(8,128)S(1)} %collective-permute-done.5, f32[7,5,32,256]{3,0,2,1:T(8,128)S(1)} %fusion.65, f32[1,7,5,32,1]{4,2,3,1,0:T(8,128)S(1)} %copy-done.4, ...), kind=kOutput, calls=%fused_computation.39 | convolution fusion | flops 26664960 | bytes 7843940 | tf_op jit(solution)/shard_map/ab,tbwl->tawl/dot_general | solution.py:90
  82.8 1.0 %fusion.131 = (f32[7,1,32,256]{3,1,2,0:T(1,128)S(1)}, f32[7,1,32,256]{3,1,2,0:T(1,128)S(1)}, f32[7,1,32,256]{3,1,2,0:T(1,128)S(1)}, f32[7,1,32,256]{3,1,2,0:T(1,128)S(1)}, f32[7,1,32,256]{3,1,2,0:T(1,128)S(1)}) fusion(f32[7,5,32,256]{3,1,2,0:T(8,128)S(1)} %fusion.20), kind=kLoop, calls=%fused_computation.207 | loop fusion | bytes 2293760 | tf_op jit(solution)/shard_map/slice | solution.py:104
  83.9 1.6 %copy_subtract_fusion.3 = f32[1,7,5,32,256]{4,2,3,1,0:T(8,128)S(1)} fusion(f32[1,7,5,32,256]{4,3,2,1,0:T(8,128)S(1)} %copy-done, f32[7,32,256]{2,1,0:T(8,128)S(1)} %bitcast.166, f32[7,32,256]{2,1,0:T(8,128)S(1)} %bitcast.167, f32[7,32,256]{2,1,0:T(8,128)S(1)} %bitcast.168, f32[7,32,256]{2,1,0:T(8,128)S(1)} %bitcast.169, f32[7,32,256]{2,1,0:T(8,128)S(1)} %bitcast.165, ...), kind=kLoop, calls=%fused_computation.5 | loop fusion | flops 2867200 | bytes 4259840 | tf_op jit(solution)/shard_map/sub | solution.py:130
  85.5 1.3 %copy.63 = f32[1,7,5,32,256]{4,3,2,1,0:T(8,128)} copy(f32[1,7,5,32,256]{4,2,3,1,0:T(8,128)S(1)} %copy_subtract_fusion.3) | data formatting | bytes 2293760 | tf_op jit(solution)/shard_map/sub | solution.py:130
  (56 shorter events, 0.5 us)
Async XLA Ops:
  1.9 11.6 %copy-start.11 = (s32[1,32]{1,0:T(1,128)S(1)}, s32[1,32]{1,0:T(1,128)}, u32[]{:S(2)}) copy-start(s32[1,32]{1,0:T(1,128)} %param.13) | copy-start | bytes 388
  2.7 33.9 %collective-permute-start.1 = (f32[7,5,2,256]{3,1,2,0:T(8,128)}, f32[7,5,2,256]{3,1,2,0:T(8,128)}, u32[]{:S(2)}, u32[]{:S(2)}) collective-permute-start(f32[7,5,2,256]{3,1,2,0:T(8,128)} %get-tuple-element.24), channel_id=1, source_target_pairs={{1,0},{2,1},{3,2},{4,3},{5,4},{6,5},{7,6},{8,7},{9,8},{10,9},{11,1... | collective-permute-start | bytes 215048 | tf_op jit(solution)/shard_map/ppermute | solution.py:30
  6.9 29.6 %collective-permute-start.2 = (f32[7,5,2,256]{3,1,2,0:T(8,128)}, f32[7,5,2,256]{3,1,2,0:T(8,128)}, u32[]{:S(2)}, u32[]{:S(2)}) collective-permute-start(f32[7,5,2,256]{3,1,2,0:T(8,128)} %get-tuple-element.25), channel_id=1, source_target_pairs={{0,1},{1,2},{2,3},{3,4},{4,5},{5,6},{6,7},{7,8},{8,9},{9,10},{10,1... | collective-permute-start | bytes 215048 | tf_op jit(solution)/shard_map/ppermute | solution.py:29
  11.4 18.2 %collective-permute-start = (f32[7,5,32]{1,0,2:T(8,128)}, f32[7,5,32]{1,0,2:T(8,128)}, u32[]{:S(2)}, u32[]{:S(2)}) collective-permute-start(f32[7,5,32]{1,0,2:T(8,128)} %bitcast.8), channel_id=1, source_target_pairs={{0,16},{1,17},{2,18},{3,19},{4,20},{5,21},{6,22},{7,23},{8,24},{9,... | collective-permute-start | bytes 13448 | tf_op jit(solution)/shard_map/ppermute | solution.py:19
  14.1 1.4 %copy-start.12 = (f32[2]{0:T(128)S(1)}, f32[2]{0:T(128)}, u32[]{:S(2)}) copy-start(f32[2]{0:T(128)} %param.11) | copy-start | bytes 28
  14.1 2.7 %copy-start.7 = (s32[2,3]{1,0:T(2,128)S(1)}, s32[2,3]{1,0:T(2,128)}, u32[]{:S(2)}) copy-start(s32[2,3]{1,0:T(2,128)} %param.10) | copy-start | bytes 76
  14.1 5.1 %copy-start.8 = (f32[7]{0:T(128)S(1)}, f32[7]{0:T(128)}, u32[]{:S(2)}) copy-start(f32[7]{0:T(128)} %constant.18.clone.1) | copy-start | bytes 88
  14.1 5.3 %copy-start = (f32[1,7,5,32,256]{4,3,2,1,0:T(8,128)S(1)}, f32[1,7,5,32,256]{4,3,2,1,0:T(8,128)}, u32[]{:S(2)}) copy-start(f32[1,7,5,32,256]{4,3,2,1,0:T(8,128)} %param.7) | copy-start | bytes 3440644
  16.8 5.7 %copy-start.6 = (f32[7,5,32]{2,0,1:T(8,128)S(1)}, f32[7,5,32]{2,0,1:T(8,128)}, u32[]{:S(2)}) copy-start(f32[7,5,32]{2,0,1:T(8,128)} %param.12) | copy-start | bytes 13444
  22.3 10.1 %copy-start.9 = (pred[32]{0:T(512)(128)(4,1)S(1)}, pred[32]{0:T(512)(128)(4,1)}, u32[]{:S(2)}) copy-start(pred[32]{0:T(512)(128)(4,1)} %compare_and_fusion) | copy-start | bytes 100
  23.3 6.3 %copy-start.5 = (f32[7,5,32]{1,0,2:T(8,128)S(1)}, f32[7,5,32]{1,0,2:T(8,128)}, u32[]{:S(2)}) copy-start(f32[7,5,32]{1,0,2:T(8,128)} %copy.39) | copy-start | bytes 13444
  42.5 1.2 %copy-start.1 = (f32[5,32,256]{2,0,1:T(8,128)S(1)}, f32[5,32,256]{2,0,1:T(8,128)}, u32[]{:S(2)}) copy-start(f32[5,32,256]{2,0,1:T(8,128)} %copy.47) | copy-start | bytes 491524
  42.5 1.2 %copy-start.2 = (f32[5,32,256]{2,0,1:T(8,128)S(1)}, f32[5,32,256]{2,0,1:T(8,128)}, u32[]{:S(2)}) copy-start(f32[5,32,256]{2,0,1:T(8,128)} %copy.46) | copy-start | bytes 491524
  42.5 1.2 %copy-start.3 = (f32[5,32,256]{2,0,1:T(8,128)S(1)}, f32[5,32,256]{2,0,1:T(8,128)}, u32[]{:S(2)}) copy-start(f32[5,32,256]{2,0,1:T(8,128)} %copy.45) | copy-start | bytes 491524
  45.6 14.2 %copy-start.4 = (f32[1,7,5,32,1]{4,2,3,1,0:T(8,128)S(1)}, f32[1,7,5,32,1]{4,2,3,1,0:T(8,128)}, u32[]{:S(2)}) copy-start(f32[1,7,5,32,1]{4,2,3,1,0:T(8,128)} %copy.41) | copy-start | bytes 13444
  45.6 14.2 %copy-start.10 = (f32[1,5,5]{2,0,1:T(1,128)S(1)}, f32[1,5,5]{2,0,1:T(1,128)}, u32[]{:S(2)}) copy-start(f32[1,5,5]{2,0,1:T(1,128)} %param.9) | copy-start | bytes 304
  45.6 9.6 %collective-permute-start.3 = (f32[7,5,2,256]{3,1,2,0:T(8,128)S(1)}, f32[7,5,2,256]{3,1,2,0:T(8,128)S(1)}, u32[]{:S(2)}, u32[]{:S(2)}) collective-permute-start(f32[7,5,2,256]{3,1,2,0:T(8,128)S(1)} %get-tuple-element.17), channel_id=1, source_target_pairs={{1,0},{2,1},{3,2},{4,3},{5,4},{6,5},{7,6},{8,7},{9,8},{10,9},{11,1... | collective-permute-start | bytes 215048 | tf_op jit(solution)/shard_map/ppermute | solution.py:30
  51.3 8.5 %collective-permute-start.4 = (f32[7,5,2,256]{3,1,2,0:T(8,128)S(1)}, f32[7,5,2,256]{3,1,2,0:T(8,128)S(1)}, u32[]{:S(2)}, u32[]{:S(2)}) collective-permute-start(f32[7,5,2,256]{3,1,2,0:T(8,128)S(1)} %get-tuple-element.18), channel_id=1, source_target_pairs={{0,1},{1,2},{2,3},{3,4},{4,5},{5,6},{6,7},{7,8},{8,9},{9,10},{10,1... | collective-permute-start | bytes 215048 | tf_op jit(solution)/shard_map/ppermute | solution.py:29
  67.6 7.9 %collective-permute-start.5 = (f32[7,5,2,256]{3,1,2,0:T(8,128)S(1)}, f32[7,5,2,256]{3,1,2,0:T(8,128)S(1)}, u32[]{:S(2)}, u32[]{:S(2)}) collective-permute-start(f32[7,5,2,256]{3,1,2,0:T(8,128)S(1)} %get-tuple-element.10), channel_id=1, source_target_pairs={{1,0},{2,1},{3,2},{4,3},{5,4},{6,5},{7,6},{8,7},{9,8},{10,9},{11,1... | collective-permute-start | bytes 215048 | tf_op jit(solution)/shard_map/ppermute | solution.py:30
  69.5 8.5 %collective-permute-start.6 = (f32[7,5,2,256]{3,1,2,0:T(8,128)S(1)}, f32[7,5,2,256]{3,1,2,0:T(8,128)S(1)}, u32[]{:S(2)}, u32[]{:S(2)}) collective-permute-start(f32[7,5,2,256]{3,1,2,0:T(8,128)S(1)} %get-tuple-element.11), channel_id=1, source_target_pairs={{0,1},{1,2},{2,3},{3,4},{4,5},{5,6},{6,7},{7,8},{8,9},{9,10},{10,1... | collective-permute-start | bytes 215048 | tf_op jit(solution)/shard_map/ppermute | solution.py:29
where the time goes:
time: 87.4 us; the launch traced here: 86.9 us
  local copies, waits for them, and re-layouts  26 us (30%)
  matrix products  22.6 us (26%)
  starting transfers between devices  22.1 us (25%)
  other arithmetic  8.68 us (10%)
  waiting for transfers between devices  7.07 us (8%)
    dot_general x3, matrix products, section_residual(): jnp.einsum('ab,tbwl->tawl', flux_jac, centre - before, precision=largest_...  15.5 us
    ppermute x3, starting transfers between devices, padded_2(): after = lax.ppermute(first, axis, down)  11.8 us
    ppermute x3, starting transfers between devices, padded_2(): before = lax.ppermute(last, axis, up)  8.17 us
    ppermute x3, waiting for transfers between devices, padded_2(): before = lax.ppermute(last, axis, up)  7.06 us
    dot_general x3, matrix products, section_residual(): jnp.einsum('ts,svwl->tvwl', spectral_derivative, centre, precision=larges...  6.51 us
    mul x4, local copies, waits for them, and re-layouts, apply_block(): inverse[None, :, column_index] * residual[:, column_index][:, None]  6.17 us
    sub x3, other arithmetic, body(): local_state - section_weight * apply_block(local_inverse, residual)  4.87 us
    slice x3, local copies, waits for them, and re-layouts, apply_block(): total = inverse[None, :, 0] * residual[:, 0][:, None]  3.13 us
  transfers between devices with their start and end apart: 7, of which 2 were waited for; matrix products, arithmetic and copies ran while one was open for 33% of the time, Pallas kernels for 0%

commit v1 on v0

v1 whole, which is shorter than its diff:
```python
import functools
import math

import jax
import jax.numpy as jnp
from jax import lax
from jax.experimental import pallas as pl
from jax.experimental.pallas import tpu as pltpu
from jax.sharding import PartitionSpec as P

SECTIONS = 3
nu_second = 0.25
nu_fourth = 0.03
time_scale = 0.05
LANES = 128
SUB = 8
PAD = 8
HALO = 2
MESH = pl.DeviceIdType.MESH


def derivative_coefficients(harm, row, samples, count):
    modes = [harm[row, j] for j in range(count)]
    result = []
    for d in range(1, samples // 2 + 1):
        total = jnp.float32(0.0)
        for n in modes:
            left = lax.rem(n, jnp.int32(samples))
            sine = jnp.float32(0.0)
            for r in range(1, count + 1):
                value = math.sin(2.0 * math.pi * ((r * d) % samples) / samples)
                sine = jnp.where(left == r, jnp.float32(value), sine)
            total = total + n.astype(jnp.float32) * sine
        result.append(total * jnp.float32(-4.0 * math.pi / samples))
    return result


def transfer_matrix(harm, upstream, delay, samples, variables, count):
    used = samples * variables
    high = -(-used // SUB) * SUB
    i = lax.broadcasted_iota(jnp.int32, (high, LANES), 0)
    j = lax.broadcasted_iota(jnp.int32, (high, LANES), 1)
    t = j // variables
    s = i // variables
    same = (i - s * variables == j - t * variables) & (i < used) & (j < used)
    total = jnp.full((high, LANES), 1.0 / samples, jnp.float32)
    for k in range(count):
        n = harm[upstream, k]
        shift = n.astype(jnp.float32) * delay
        steps = n * (t - s + samples)
        steps = steps - samples * (steps // samples)
        turns = steps.astype(jnp.float32) * (1.0 / samples) + shift
        turns = turns - jnp.floor(turns)
        total = total + (2.0 / samples) * jnp.cos((2.0 * math.pi) * turns)
    total = jnp.where(same, total, 0.0)
    return jnp.concatenate([total, jnp.zeros((LANES - high, LANES), jnp.float32)], axis=0)


def kernel(rows, n, samples, variables, count,
           state, inverse, flux, harm, delay, inflow, pairing, out,
           q0, qa, qb, iv, ghost, mixing, xout, xin, flow, send, recv,
           load_sem, iv_sem, out_sem, send_sem, recv_sem, xsend_sem, xrecv_sem):
    halves, _, _, lines, _ = iv.shape[0], iv.shape[1], iv.shape[2], iv.shape[3], iv.shape[4]
    tv = samples * variables
    tiles = lines // SUB
    row = lax.axis_index("row")
    me = lax.axis_index("mesh")
    has_down = me > 0
    has_up = me < n - 1
    has_before = row > 0
    has_after = row < rows - 1
    down, up, before, after = {"mesh": me - 1}, {"mesh": me + 1}, {"row": row - 1}, {"row": row + 1}
    ways = ((has_down, down), (has_up, up), (has_before, before), (has_after, after))

    barrier = pltpu.get_barrier_semaphore()
    for ok, where in ways:
        @pl.when(ok)
        def _(where=where):
            pl.semaphore_signal(barrier, inc=1, device_id=where, device_id_type=MESH)

    loads = [
        pltpu.make_async_copy(
            state.at[:, :, pl.ds(h * LANES, LANES)],
            q0.at[h, :, pl.ds(PAD, lines), :],
            load_sem.at[h],
        )
        for h in range(halves)
    ]
    iv_loads = [
        pltpu.make_async_copy(
            inverse.at[:, :, :, pl.ds(h * LANES, LANES)], iv.at[h], iv_sem.at[h]
        )
        for h in range(halves)
    ]
    for copy in reversed(loads):
        copy.start()
    for copy in iv_loads:
        copy.start()

    zeros = jnp.zeros((tv, PAD, LANES), jnp.float32)
    for q in (qa, qb, q0):
        for h in range(halves):
            q[h, :, 0:PAD, :] = zeros
            q[h, :, PAD + lines : 2 * PAD + lines, :] = zeros

    for copy in reversed(loads):
        copy.wait()

    lane = lax.broadcasted_iota(jnp.int32, (lines, LANES), 1)
    packed = jnp.zeros((lines, LANES), jnp.float32)
    for i in range(tv):
        column = pltpu.roll(q0[halves - 1, i, PAD : PAD + lines, :], (i + 1) % LANES, 1)
        packed = jnp.where(lane == i, column, packed)
    xout[...] = packed

    def copies(s):
        first = pltpu.make_async_remote_copy(
            src_ref=send.at[s, 0], dst_ref=recv.at[s, 1], send_sem=send_sem.at[s, 0],
            recv_sem=recv_sem.at[s, 1], device_id=down, device_id_type=MESH)
        last = pltpu.make_async_remote_copy(
            src_ref=send.at[s, 1], dst_ref=recv.at[s, 0], send_sem=send_sem.at[s, 1],
            recv_sem=recv_sem.at[s, 0], device_id=up, device_id_type=MESH)
        return first, last

    def pack(s, q):
        for h in range(halves):
            send[s, 0, h] = q[h, :, PAD : PAD + HALO, :]
            send[s, 1, h] = q[h, :, PAD + lines - HALO : PAD + lines, :]

    def start(s):
        first, last = copies(s)
        pl.when(has_down)(first.start)
        pl.when(has_up)(last.start)

    def finish(s, q):
        first, last = copies(s)

        @pl.when(has_down)
        def _():
            last.wait_recv()
            for h in range(halves):
                q[h, :, PAD - HALO : PAD, :] = recv[s, 0, h]

        @pl.when(has_up)
        def _():
            first.wait_recv()
            for h in range(halves):
                q[h, :, PAD + lines : PAD + lines + HALO, :] = recv[s, 1, h]

    pack(0, q0)
    across = pltpu.make_async_remote_copy(
        src_ref=xout, dst_ref=xin, send_sem=xsend_sem, recv_sem=xrecv_sem,
        device_id=after, device_id_type=MESH)

    greeted = sum(ok.astype(jnp.int32) for ok, _ in ways)
    pl.semaphore_wait(barrier, greeted)
    pl.when(has_after)(across.start)
    start(0)

    weights = [(s + 1.0) / SECTIONS for s in range(SECTIONS)]
    for s in range(SECTIONS):
        for b in range(variables):
            for a in range(variables):
                mixing[s, b, a] = jnp.full((SUB, LANES), flux[0, a, b] * jnp.float32(weights[s]), jnp.float32)
    slopes = derivative_coefficients(harm, row, samples, count)
    to_ghost = transfer_matrix(harm, jnp.maximum(row - 1, 0), delay[row], samples, variables, count)
    chosen = (
        jnp.broadcast_to(pairing[...] - me * lines, (lines, lines))
        == lax.broadcasted_iota(jnp.int32, (lines, lines), 0)
    ).astype(jnp.float32)

    @pl.when(row == 0)
    def _():
        flow[...] = jnp.zeros((LANES, LANES), jnp.float32)
        for t in range(samples):
            flow[t * variables : (t + 1) * variables, 0:lines] = inflow[t]
        xin[...] = jnp.transpose(flow[...])[0:lines, :]

    @pl.when(has_before)
    def _():
        across.wait_recv()

    paired = lax.dot_general(
        chosen, xin[...], (((0,), (0,)), ((), ())),
        precision=lax.Precision.HIGHEST, preferred_element_type=jnp.float32)
    shifted = jnp.dot(
        paired, to_ghost, precision=lax.Precision.HIGHEST, preferred_element_type=jnp.float32)
    for i in range(tv):
        ghost[i] = pltpu.roll(shifted, (LANES - i) % LANES, 1)
    for copy in iv_loads:
        copy.wait()

    at_start = lax.broadcasted_iota(jnp.int32, (variables, SUB, LANES), 2) == 0

    def tile(s, k, src, dst):
        w = weights[s]
        k0 = jnp.float32(w * (2.0 * nu_second + 6.0 * nu_fourth))
        k1 = jnp.float32(w * (-nu_second - 4.0 * nu_fourth))
        k2 = jnp.float32(w * nu_fourth)
        turn = [e * jnp.float32(time_scale * w) for e in slopes]
        base = pl.multiple_of(PAD + k * SUB, SUB)
        line = pl.multiple_of(k * SUB, SUB)
        for t in range(samples):
            own = pl.ds(t * variables, variables)
            lower = ghost[own, pl.ds(line, SUB), :]
            for h in range(halves):
                centre = src[h, own, pl.ds(base, SUB), :]
                rolled = pltpu.roll(centre, 1, 2)
                step = centre - jnp.where(at_start, lower, rolled)
                lower = rolled
                total = k0 * centre
                total = total + k1 * (src[h, own, pl.ds(base - 1, SUB), :] + src[h, own, pl.ds(base + 1, SUB), :])
                total = total + k2 * (src[h, own, pl.ds(base - 2, SUB), :] + src[h, own, pl.ds(base + 2, SUB), :])
                for d, slope in enumerate(turn, 1):
                    earlier = pl.ds(((t - d) % samples) * variables, variables)
                    later = pl.ds(((t + d) % samples) * variables, variables)
                    total = total + slope * (
                        src[h, earlier, pl.ds(base, SUB), :] - src[h, later, pl.ds(base, SUB), :])
                for b in range(variables):
                    total = total + mixing[s, b] * step[b : b + 1]
                new = q0[h, own, pl.ds(base, SUB), :]
                for c in range(variables):
                    new = new - iv[h, :, c, pl.ds(line, SUB), :] * total[c : c + 1]
                dst[h, own, pl.ds(base, SUB), :] = new

    def inner(s, src, dst):
        @pl.loop(1, tiles - 1)
        def _(k):
            tile(s, k, src, dst)

    def outer(s, src, dst):
        @pl.loop(0, 2)
        def _(i):
            tile(s, i * (tiles - 1), src, dst)

    inner(0, q0, qa)
    finish(0, q0)
    outer(0, q0, qa)
    pack(1, qa)
    start(1)
    inner(1, qa, qb)
    finish(1, qa)
    outer(1, qa, qb)
    pack(2, qb)
    start(2)
    inner(2, qb, qa)
    finish(2, qb)
    outer(2, qb, qa)

    stores = [
        pltpu.make_async_copy(
            qa.at[h, :, pl.ds(PAD, lines), :],
            out.at[:, :, pl.ds(h * LANES, LANES)],
            out_sem.at[h],
        )
        for h in range(halves)
    ]
    for copy in stores:
        copy.start()
    for s in range(SECTIONS):
        first, last = copies(s)
        pl.when(has_down)(first.wait_send)
        pl.when(has_up)(last.wait_send)
    pl.when(has_after)(across.wait_send)
    for copy in stores:
        copy.wait()


def body(rows, n, state, inverse_blocks, flux_jacobian, harmonics, interface_delay, inflow, pairing):
    _, samples, variables, lines, cells = state.shape
    count = harmonics.shape[1]
    tv = samples * variables
    halves = cells // LANES
    padded = (halves, tv, lines + 2 * PAD, LANES)
    smem = pl.BlockSpec(memory_space=pltpu.SMEM)
    vmem = pl.BlockSpec(memory_space=pltpu.VMEM)
    hbm = pl.BlockSpec(memory_space=pl.ANY)
    f32 = jnp.float32
    work = SECTIONS * 40 * tv * lines * cells
    moved = 4 * lines * cells * (2 * tv + variables * variables)
    result = pl.pallas_call(
        functools.partial(kernel, rows, n, samples, variables, count),
        out_shape=jax.ShapeDtypeStruct((tv, lines, cells), f32),
        in_specs=[hbm, hbm, smem, smem, smem, vmem, vmem],
        out_specs=hbm,
        scratch_shapes=[
            pltpu.VMEM(padded, f32),
            pltpu.VMEM(padded, f32),
            pltpu.VMEM(padded, f32),
            pltpu.VMEM((halves, variables, variables, lines, LANES), f32),
            pltpu.VMEM((tv, lines, LANES), f32),
            pltpu.VMEM((SECTIONS, variables, variables, SUB, LANES), f32),
            pltpu.VMEM((lines, LANES), f32),
            pltpu.VMEM((lines, LANES), f32),
            pltpu.VMEM((LANES, LANES), f32),
            pltpu.VMEM((SECTIONS, 2, halves, tv, HALO, LANES), f32),
            pltpu.VMEM((SECTIONS, 2, halves, tv, HALO, LANES), f32),
            pltpu.SemaphoreType.DMA((halves,)),
            pltpu.SemaphoreType.DMA((halves,)),
            pltpu.SemaphoreType.DMA((halves,)),
            pltpu.SemaphoreType.DMA((SECTIONS, 2)),
            pltpu.SemaphoreType.DMA((SECTIONS, 2)),
            pltpu.SemaphoreType.DMA,
            pltpu.SemaphoreType.DMA,
        ],
        compiler_params=pltpu.CompilerParams(
            collective_id=0, has_side_effects=True, vmem_limit_bytes=32 * 1024 * 1024),
        cost_estimate=pl.CostEstimate(flops=work, bytes_accessed=moved, transcendentals=0),
    )(
        state.reshape(tv, lines, cells),
        inverse_blocks.reshape(variables, variables, lines, cells),
        flux_jacobian, harmonics, interface_delay, inflow, pairing,
    )
    return result.reshape(state.shape)


def solution(mesh):
    return jax.shard_map(
        functools.partial(body, mesh.shape["row"], mesh.shape["mesh"]),
        mesh=mesh,
        in_specs=(
            P("row", None, None, "mesh", None),
            P("row", None, None, "mesh", None),
            P("row", None, None),
            P(),
            P(),
            P(None, None, "mesh"),
            P("row", "mesh"),
        ),
        out_specs=P("row", None, None, "mesh", None),
        check_vma=False,
    )
```

time: 87.4 us -> 26.2 us (0.30)
  matrix products: 22.6 us -> 0 us
  starting transfers between devices: 22.1 us -> 0 us
  local copies, waits for them, and re-layouts: 26 us -> 6.81 us
  Pallas kernels: 0 us -> 18.9 us
  other arithmetic: 8.68 us -> 0 us
  waiting for transfers between devices: 7.07 us -> 0 us
    dot_general x9 -> x0, matrix products: 22.6 us -> none  [the longest x3 15.5 us: section_residual(): jnp.einsum('ab,tbwl->tawl', flux_jac, centre - before, precision=largest_...]
    ppermute x7 -> x0, starting transfers between devices: 22.1 us -> none  [the longest x3 11.8 us: padded_2(): after = lax.ppermute(first, axis, down)]
    pallas_call x0 -> x1, Pallas kernels: none -> 18.9 us  [body(): pl.pallas_call(functools.partial(kernel, rows, n, samples, variables, cou...]
    mul x6 -> x0, local copies, waits for them, and re-layouts: 8.37 us -> none  [the longest x4 6.17 us: apply_block(): inverse[None, :, column_index] * residual[:, column_index][:, None]]
    ppermute x7 -> x0, waiting for transfers between devices: 7.07 us -> none  [the longest x3 7.06 us: padded_2(): before = lax.ppermute(last, axis, up)]
    sub x3 -> x0, other arithmetic: 4.87 us -> none  [body(): local_state - section_weight * apply_block(local_inverse, residual)]
    slice x7 -> x0, local copies, waits for them, and re-layouts: 4.19 us -> none  [the longest x3 3.13 us: apply_block(): total = inverse[None, :, 0] * residual[:, 0][:, None]]
    unnamed x43 -> x13, local copies, waits for them, and re-layouts: 3.03 us -> 6.81 us
  transfers between devices with their start and end apart: 7 -> 0, of which waited for: 2 -> 0; matrix products, arithmetic and copies ran while one was open for 33% -> 0% of each run, Pallas kernels for 0% -> 0%
where the time goes in v1:
time: 26.2 us; the launch traced here: 25.8 us
  Pallas kernels  18.9 us (72%)
  local copies, waits for them, and re-layouts  6.81 us (26%)
    pallas_call x1, Pallas kernels, body(): pl.pallas_call(functools.partial(kernel, rows, n, samples, variables, cou...  18.9 us
    unnamed x13, local copies, waits for them, and re-layouts  6.81 us

profile of v1, /device:TPU:24, one launch (start us, length us, event | category | flops | bytes accessed | tf_op | source)
XLA Modules:
  0.0 25.8 jit_solution(6260593444982375402)
XLA Ops:
  0.0 0.7 %copy.8.flux = f32[1,5,5]{2,1,0:T(8,128)S(1)} copy(f32[1,5,5]{2,0,1:T(1,128)} %param.9) | data formatting | bytes 200 | tf_op args[2]
  0.7 0.7 %copy.9.inflow = f32[7,5,32]{2,1,0:T(8,128)S(1)} copy(f32[7,5,32]{2,0,1:T(8,128)} %param.12) | data formatting | bytes 8960 | tf_op args[5]
  1.4 0.0 copy-start
  1.4 1.3 %copy-done = f32[1,7,5,32,256]{4,3,2,1,0:T(8,128)S(1)} copy-done((f32[1,7,5,32,256]{4,3,2,1,0:T(8,128)S(1)}, f32[1,7,5,32,256]{4,3,2,1,0:T(8,128)}, u32[]{:S(2)}) %copy-start) | copy-done | bytes 1146904
  2.7 0.0 copy-start.1
  2.7 1.1 %copy-done.1 = f32[1,5,5,32,256]{4,3,2,1,0:T(8,128)S(1)} copy-done((f32[1,5,5,32,256]{4,3,2,1,0:T(8,128)S(1)}, f32[1,5,5,32,256]{4,3,2,1,0:T(8,128)}, u32[]{:S(2)}) %copy-start.1) | copy-done | bytes 819224
  3.8 0.0 copy-start.2
  3.8 0.7 %copy-done.2 = s32[2,3]{1,0:T(2,128)S(1)} copy-done((s32[2,3]{1,0:T(2,128)S(1)}, s32[2,3]{1,0:T(2,128)}, u32[]{:S(2)}) %copy-start.2) | copy-done | bytes 48
  4.5 0.0 copy-start.3
  4.5 0.7 %copy-done.3 = f32[2]{0:T(128)S(1)} copy-done((f32[2]{0:T(128)S(1)}, f32[2]{0:T(128)}, u32[]{:S(2)}) %copy-start.3) | copy-done | bytes 32
  5.2 0.0 copy-start.4
  5.2 0.7 %copy-done.4 = s32[1,32]{1,0:T(1,128)S(1)} copy-done((s32[1,32]{1,0:T(1,128)S(1)}, s32[1,32]{1,0:T(1,128)}, u32[]{:S(2)}) %copy-start.4) | copy-done | bytes 152
  5.8 18.9 %shard_map.73 = f32[35,32,256]{2,1,0:T(8,128)S(1)} custom-call(f32[35,32,256]{2,1,0:T(8,128)S(1)} %bitcast.4, f32[5,5,32,256]{3,2,1,0:T(8,128)S(1)} %bitcast.5, f32[1,5,5]{2,1,0:T(8,128)S(1)} %copy.8.flux, s32[2,3]{1,0:T(2,128)S(1)} %copy-done.2, f32[2]{0:T(128)S(1)} %copy-done.3, f32[7,5,32]{2,1,0:T(8,128)S(1)} %copy.9.inflow, s32[1,32]{1,0:T(1,128)S(1)} %copy-done.4), custom_call_target="tpu_custom_call" | custom-call | flops 34406400 | bytes 3112960 | tf_op jit(solution)/shard_map/pallas_call | solution.py:281
  24.8 1.0 %copy.11 = f32[1,7,5,32,256]{4,3,2,1,0:T(8,128)} copy(f32[1,7,5,32,256]{4,3,2,1,0:T(8,128)S(1)} %bitcast.3) | data formatting | bytes 2293760
Async XLA Ops:
  1.4 1.3 %copy-start = (f32[1,7,5,32,256]{4,3,2,1,0:T(8,128)S(1)}, f32[1,7,5,32,256]{4,3,2,1,0:T(8,128)}, u32[]{:S(2)}) copy-start(f32[1,7,5,32,256]{4,3,2,1,0:T(8,128)} %param.7) | copy-start | bytes 3440644
  2.7 1.1 %copy-start.1 = (f32[1,5,5,32,256]{4,3,2,1,0:T(8,128)S(1)}, f32[1,5,5,32,256]{4,3,2,1,0:T(8,128)}, u32[]{:S(2)}) copy-start(f32[1,5,5,32,256]{4,3,2,1,0:T(8,128)} %param.8) | copy-start | bytes 2457604
  3.8 0.7 %copy-start.2 = (s32[2,3]{1,0:T(2,128)S(1)}, s32[2,3]{1,0:T(2,128)}, u32[]{:S(2)}) copy-start(s32[2,3]{1,0:T(2,128)} %harm.1) | copy-start | bytes 76
  4.5 0.7 %copy-start.3 = (f32[2]{0:T(128)S(1)}, f32[2]{0:T(128)}, u32[]{:S(2)}) copy-start(f32[2]{0:T(128)} %delay.1) | copy-start | bytes 28
  5.2 0.7 %copy-start.4 = (s32[1,32]{1,0:T(1,128)S(1)}, s32[1,32]{1,0:T(1,128)}, u32[]{:S(2)}) copy-start(s32[1,32]{1,0:T(1,128)} %pairing.1) | copy-start | bytes 388

commit v2 on v1

--- a/solution.py
+++ b/solution.py
@@ -57,9 +57,10 @@
 
 
 def kernel(rows, n, samples, variables, count,
-           state, inverse, flux, harm, delay, inflow, pairing, out,
+           state, inverse, flux_hbm, harm_hbm, delay_hbm, inflow_hbm, pairing_hbm, out,
            q0, qa, qb, iv, ghost, mixing, xout, xin, flow, send, recv,
-           load_sem, iv_sem, out_sem, send_sem, recv_sem, xsend_sem, xrecv_sem):
+           flux, harm, delay, inflow, pairing, final,
+           load_sem, iv_sem, small_sem, out_sem, send_sem, recv_sem, xsend_sem, xrecv_sem):
     halves, _, _, lines, _ = iv.shape[0], iv.shape[1], iv.shape[2], iv.shape[3], iv.shape[4]
     tv = samples * variables
     tiles = lines // SUB
@@ -92,9 +93,15 @@
         )
         for h in range(halves)
     ]
+    small = [
+        pltpu.make_async_copy(source, target, small_sem.at[i])
+        for i, (source, target) in enumerate((
+            (flux_hbm, flux), (harm_hbm, harm), (delay_hbm, delay),
+            (inflow_hbm, inflow), (pairing_hbm, pairing)))
+    ]
     for copy in reversed(loads):
         copy.start()
-    for copy in iv_loads:
+    for copy in small + iv_loads:
         copy.start()
 
     zeros = jnp.zeros((tv, PAD, LANES), jnp.float32)
@@ -122,32 +129,36 @@
             recv_sem=recv_sem.at[s, 0], device_id=up, device_id_type=MESH)
         return first, last
 
-    def pack(s, q):
+    def pack_down(s, q):
         for h in range(halves):
             send[s, 0, h] = q[h, :, PAD : PAD + HALO, :]
+
+    def pack_up(s, q):
+        for h in range(halves):
             send[s, 1, h] = q[h, :, PAD + lines - HALO : PAD + lines, :]
 
-    def start(s):
-        first, last = copies(s)
-        pl.when(has_down)(first.start)
-        pl.when(has_up)(last.start)
-
-    def finish(s, q):
-        first, last = copies(s)
-
+    def start_down(s):
+        pl.when(has_down)(copies(s)[0].start)
+
+    def start_up(s):
+        pl.when(has_up)(copies(s)[1].start)
+
+    def finish_down(s, q):
         @pl.when(has_down)
         def _():
-            last.wait_recv()
+            copies(s)[1].wait_recv()
             for h in range(halves):
                 q[h, :, PAD - HALO : PAD, :] = recv[s, 0, h]
 
+    def finish_up(s, q):
         @pl.when(has_up)
         def _():
-            first.wait_recv()
+            copies(s)[0].wait_recv()
             for h in range(halves):
                 q[h, :, PAD + lines : PAD + lines + HALO, :] = recv[s, 1, h]
 
-    pack(0, q0)
+    pack_down(0, q0)
+    pack_up(0, q0)
     across = pltpu.make_async_remote_copy(
         src_ref=xout, dst_ref=xin, send_sem=xsend_sem, recv_sem=xrecv_sem,
         device_id=after, device_id_type=MESH)
@@ -155,13 +166,16 @@
     greeted = sum(ok.astype(jnp.int32) for ok, _ in ways)
     pl.semaphore_wait(barrier, greeted)
     pl.when(has_after)(across.start)
-    start(0)
-
+    start_down(0)
+    start_up(0)
+
+    for copy in small:
+        copy.wait()
     weights = [(s + 1.0) / SECTIONS for s in range(SECTIONS)]
     for s in range(SECTIONS):
         for b in range(variables):
             for a in range(variables):
-                mixing[s, b, a] = jnp.full((SUB, LANES), flux[0, a, b] * jnp.float32(weights[s]), jnp.float32)
+                mixing[s, b, a] = jnp.full((SUB, LANES), flux[a, 0, b] * jnp.float32(weights[s]), jnp.float32)
     slopes = derivative_coefficients(harm, row, samples, count)
     to_ghost = transfer_matrix(harm, jnp.maximum(row - 1, 0), delay[row], samples, variables, count)
     chosen = (
@@ -173,7 +187,8 @@
     def _():
         flow[...] = jnp.zeros((LANES, LANES), jnp.float32)
         for t in range(samples):
-            flow[t * variables : (t + 1) * variables, 0:lines] = inflow[t]
+            for v in range(variables):
+                flow[t * variables + v : t * variables + v + 1, 0:lines] = inflow[v, t : t + 1]
         xin[...] = jnp.transpose(flow[...])[0:lines, :]
 
     @pl.when(has_before)
@@ -198,8 +213,9 @@
         k1 = jnp.float32(w * (-nu_second - 4.0 * nu_fourth))
         k2 = jnp.float32(w * nu_fourth)
         turn = [e * jnp.float32(time_scale * w) for e in slopes]
-        base = pl.multiple_of(PAD + k * SUB, SUB)
-        line = pl.multiple_of(k * SUB, SUB)
+        line, base = k * SUB, PAD + k * SUB
+        if not isinstance(k, int):
+            line, base = pl.multiple_of(line, SUB), pl.multiple_of(base, SUB)
         for t in range(samples):
             own = pl.ds(t * variables, variables)
             lower = ghost[own, pl.ds(line, SUB), :]
@@ -221,42 +237,42 @@
                 new = q0[h, own, pl.ds(base, SUB), :]
                 for c in range(variables):
                     new = new - iv[h, :, c, pl.ds(line, SUB), :] * total[c : c + 1]
-                dst[h, own, pl.ds(base, SUB), :] = new
-
-    def inner(s, src, dst):
+                if dst is None:
+                    final[own, pl.ds(line, SUB), h * LANES : (h + 1) * LANES] = new
+                else:
+                    dst[h, own, pl.ds(base, SUB), :] = new
+
+    stores = [
+        pltpu.make_async_copy(final.at[:, part, :], out.at[:, part, :], out_sem.at[i])
+        for i, part in enumerate((pl.ds(SUB, lines - 2 * SUB), pl.ds(0, SUB), pl.ds(lines - SUB, SUB)))
+    ]
+
+    def section(s, src, dst):
         @pl.loop(1, tiles - 1)
         def _(k):
             tile(s, k, src, dst)
 
-    def outer(s, src, dst):
-        @pl.loop(0, 2)
-        def _(i):
-            tile(s, i * (tiles - 1), src, dst)
-
-    inner(0, q0, qa)
-    finish(0, q0)
-    outer(0, q0, qa)
-    pack(1, qa)
-    start(1)
-    inner(1, qa, qb)
-    finish(1, qa)
-    outer(1, qa, qb)
-    pack(2, qb)
-    start(2)
-    inner(2, qb, qa)
-    finish(2, qb)
-    outer(2, qb, qa)
-
-    stores = [
-        pltpu.make_async_copy(
-            qa.at[h, :, pl.ds(PAD, lines), :],
-            out.at[:, :, pl.ds(h * LANES, LANES)],
-            out_sem.at[h],
-        )
-        for h in range(halves)
-    ]
-    for copy in stores:
-        copy.start()
+        if dst is None:
+            stores[0].start()
+        finish_down(s, src)
+        tile(s, 0, src, dst)
+        if dst is None:
+            stores[1].start()
+        if s < SECTIONS - 1:
+            pack_down(s + 1, dst)
+            start_down(s + 1)
+        finish_up(s, src)
+        tile(s, tiles - 1, src, dst)
+        if dst is None:
+            stores[2].start()
+        if s < SECTIONS - 1:
+            pack_up(s + 1, dst)
+            start_up(s + 1)
+
+    section(0, q0, qa)
+    section(1, qa, qb)
+    section(2, qb, None)
+
     for s in range(SECTIONS):
         first, last = copies(s)
         pl.when(has_down)(first.wait_send)
@@ -272,16 +288,14 @@
     tv = samples * variables
     halves = cells // LANES
     padded = (halves, tv, lines + 2 * PAD, LANES)
-    smem = pl.BlockSpec(memory_space=pltpu.SMEM)
-    vmem = pl.BlockSpec(memory_space=pltpu.VMEM)
-    hbm = pl.BlockSpec(memory_space=pl.ANY)
+    hbm = pl.BlockSpec(memory_space=pltpu.HBM)
     f32 = jnp.float32
     work = SECTIONS * 40 * tv * lines * cells
     moved = 4 * lines * cells * (2 * tv + variables * variables)
     result = pl.pallas_call(
         functools.partial(kernel, rows, n, samples, variables, count),
         out_shape=jax.ShapeDtypeStruct((tv, lines, cells), f32),
-        in_specs=[hbm, hbm, smem, smem, smem, vmem, vmem],
+        in_specs=[hbm] * 7,
         out_specs=hbm,
         scratch_shapes=[
             pltpu.VMEM(padded, f32),
@@ -295,21 +309,29 @@
             pltpu.VMEM((LANES, LANES), f32),
             pltpu.VMEM((SECTIONS, 2, halves, tv, HALO, LANES), f32),
             pltpu.VMEM((SECTIONS, 2, halves, tv, HALO, LANES), f32),
+            pltpu.SMEM((variables, 1, variables), f32),
+            pltpu.SMEM(harmonics.shape, jnp.int32),
+            pltpu.SMEM(interface_delay.shape, f32),
+            pltpu.VMEM((variables, samples, lines), f32),
+            pltpu.VMEM(pairing.shape, jnp.int32),
+            pltpu.VMEM((tv, lines, cells), f32),
             pltpu.SemaphoreType.DMA((halves,)),
             pltpu.SemaphoreType.DMA((halves,)),
-            pltpu.SemaphoreType.DMA((halves,)),
+            pltpu.SemaphoreType.DMA((5,)),
+            pltpu.SemaphoreType.DMA((3,)),
             pltpu.SemaphoreType.DMA((SECTIONS, 2)),
             pltpu.SemaphoreType.DMA((SECTIONS, 2)),
             pltpu.SemaphoreType.DMA,
             pltpu.SemaphoreType.DMA,
         ],
         compiler_params=pltpu.CompilerParams(
-            collective_id=0, has_side_effects=True, vmem_limit_bytes=32 * 1024 * 1024),
+            collective_id=0, has_side_effects=True),
         cost_estimate=pl.CostEstimate(flops=work, bytes_accessed=moved, transcendentals=0),
     )(
         state.reshape(tv, lines, cells),
         inverse_blocks.reshape(variables, variables, lines, cells),
-        flux_jacobian, harmonics, interface_delay, inflow, pairing,
+        jnp.transpose(flux_jacobian, (1, 0, 2)), harmonics, interface_delay,
+        jnp.transpose(inflow, (1, 0, 2)), pairing,
     )
     return result.reshape(state.shape)
 

time: 26.2 us -> 21.9 us (0.84)
  local copies, waits for them, and re-layouts: 6.81 us -> 2.39 us
  Pallas kernels: 18.9 us -> 19.3 us
    unnamed x13 -> x1, local copies, waits for them, and re-layouts: 6.81 us -> 2.39 us
    pallas_call x1, Pallas kernels: 18.9 us -> 19.3 us  [body(): pl.pallas_call(functools.partial(kernel, rows, n, samples, variables, cou...]
where the time goes in v2:
time: 21.9 us; the launch traced here: 21.7 us
  Pallas kernels  19.3 us (88%)
  local copies, waits for them, and re-layouts  2.39 us (11%)
    pallas_call x1, Pallas kernels, body(): pl.pallas_call(functools.partial(kernel, rows, n, samples, variables, cou...  19.3 us
    unnamed x1, local copies, waits for them, and re-layouts  2.39 us

profile of v2, /device:TPU:24, one launch (start us, length us, event | category | flops | bytes accessed | tf_op | source)
XLA Modules:
  0.0 21.7 jit_solution(10968780642142650688)
XLA Ops:
  0.0 19.3 %shard_map.73 = f32[35,32,256]{2,1,0:T(8,128)} custom-call(f32[35,32,256]{2,1,0:T(8,128)} %bitcast.6, f32[5,5,32,256]{3,2,1,0:T(8,128)} %bitcast.7, f32[5,1,5]{2,1,0:T(1,128)} %bitcast.9, s32[2,3]{1,0:T(2,128)} %harm_hbm.1, f32[2]{0:T(128)} %delay_hbm.1, f32[5,7,32]{2,1,0:T(8,128)} %bitcast.8, s32[1,32]{1,0:T(1,128)} %pairing_hbm.1), custom_call_target="tpu_custom_call" | custom-call | flops 34406400 | bytes 3112960 | tf_op jit(solution)/shard_map/pallas_call | solution.py:295
  19.3 2.4 %copy.9 = f32[1,7,5,32,256]{4,3,2,1,0:T(8,128)} copy(f32[1,7,5,32,256]{4,3,2,1,0:T(8,128)} %bitcast.5) | data formatting | bytes 2293760

commit v3 on v2

--- a/solution.py
+++ b/solution.py
@@ -59,9 +59,9 @@
 def kernel(rows, n, samples, variables, count,
            state, inverse, flux_hbm, harm_hbm, delay_hbm, inflow_hbm, pairing_hbm, out,
            q0, qa, qb, iv, ghost, mixing, xout, xin, flow, send, recv,
-           flux, harm, delay, inflow, pairing, final,
-           load_sem, iv_sem, small_sem, out_sem, send_sem, recv_sem, xsend_sem, xrecv_sem):
-    halves, _, _, lines, _ = iv.shape[0], iv.shape[1], iv.shape[2], iv.shape[3], iv.shape[4]
+           flux, harm, delay, inflow, pairing,
+           load_sem, iv_sem, small_sem, send_sem, recv_sem, xsend_sem, xrecv_sem):
+    halves, _, _, lines, _ = iv.shape
     tv = samples * variables
     tiles = lines // SUB
     row = lax.axis_index("row")
@@ -104,21 +104,8 @@
     for copy in small + iv_loads:
         copy.start()
 
-    zeros = jnp.zeros((tv, PAD, LANES), jnp.float32)
-    for q in (qa, qb, q0):
-        for h in range(halves):
-            q[h, :, 0:PAD, :] = zeros
-            q[h, :, PAD + lines : 2 * PAD + lines, :] = zeros
-
     for copy in reversed(loads):
         copy.wait()
-
-    lane = lax.broadcasted_iota(jnp.int32, (lines, LANES), 1)
-    packed = jnp.zeros((lines, LANES), jnp.float32)
-    for i in range(tv):
-        column = pltpu.roll(q0[halves - 1, i, PAD : PAD + lines, :], (i + 1) % LANES, 1)
-        packed = jnp.where(lane == i, column, packed)
-    xout[...] = packed
 
     def copies(s):
         first = pltpu.make_async_remote_copy(
@@ -165,9 +152,21 @@
 
     greeted = sum(ok.astype(jnp.int32) for ok, _ in ways)
     pl.semaphore_wait(barrier, greeted)
-    pl.when(has_after)(across.start)
     start_down(0)
     start_up(0)
+    lane = lax.broadcasted_iota(jnp.int32, (lines, LANES), 1)
+    packed = jnp.zeros((lines, LANES), jnp.float32)
+    for i in range(tv):
+        column = pltpu.roll(q0[halves - 1, i, PAD : PAD + lines, :], (i + 1) % LANES, 1)
+        packed = jnp.where(lane == i, column, packed)
+    xout[...] = packed
+    pl.when(has_after)(across.start)
+
+    zeros = jnp.zeros((tv, PAD, LANES), jnp.float32)
+    for q in (qa, qb, q0):
+        for h in range(halves):
+            q[h, :, 0:PAD, :] = zeros
+            q[h, :, PAD + lines : 2 * PAD + lines, :] = zeros
 
     for copy in small:
         copy.wait()
@@ -238,33 +237,22 @@
                 for c in range(variables):
                     new = new - iv[h, :, c, pl.ds(line, SUB), :] * total[c : c + 1]
                 if dst is None:
-                    final[own, pl.ds(line, SUB), h * LANES : (h + 1) * LANES] = new
+                    out[own, pl.ds(line, SUB), h * LANES : (h + 1) * LANES] = new
                 else:
                     dst[h, own, pl.ds(base, SUB), :] = new
-
-    stores = [
-        pltpu.make_async_copy(final.at[:, part, :], out.at[:, part, :], out_sem.at[i])
-        for i, part in enumerate((pl.ds(SUB, lines - 2 * SUB), pl.ds(0, SUB), pl.ds(lines - SUB, SUB)))
-    ]
 
     def section(s, src, dst):
         @pl.loop(1, tiles - 1)
         def _(k):
             tile(s, k, src, dst)
 
-        if dst is None:
-            stores[0].start()
         finish_down(s, src)
         tile(s, 0, src, dst)
-        if dst is None:
-            stores[1].start()
         if s < SECTIONS - 1:
             pack_down(s + 1, dst)
             start_down(s + 1)
         finish_up(s, src)
         tile(s, tiles - 1, src, dst)
-        if dst is None:
-            stores[2].start()
         if s < SECTIONS - 1:
             pack_up(s + 1, dst)
             start_up(s + 1)
@@ -278,8 +266,6 @@
         pl.when(has_down)(first.wait_send)
         pl.when(has_up)(last.wait_send)
     pl.when(has_after)(across.wait_send)
-    for copy in stores:
-        copy.wait()
 
 
 def body(rows, n, state, inverse_blocks, flux_jacobian, harmonics, interface_delay, inflow, pairing):
@@ -294,9 +280,9 @@
     moved = 4 * lines * cells * (2 * tv + variables * variables)
     result = pl.pallas_call(
         functools.partial(kernel, rows, n, samples, variables, count),
-        out_shape=jax.ShapeDtypeStruct((tv, lines, cells), f32),
+        out_shape=pltpu.VMEM((tv, lines, cells), f32),
         in_specs=[hbm] * 7,
-        out_specs=hbm,
+        out_specs=pl.BlockSpec(memory_space=pltpu.VMEM),
         scratch_shapes=[
             pltpu.VMEM(padded, f32),
             pltpu.VMEM(padded, f32),
@@ -314,11 +300,9 @@
             pltpu.SMEM(interface_delay.shape, f32),
             pltpu.VMEM((variables, samples, lines), f32),
             pltpu.VMEM(pairing.shape, jnp.int32),
-            pltpu.VMEM((tv, lines, cells), f32),
             pltpu.SemaphoreType.DMA((halves,)),
             pltpu.SemaphoreType.DMA((halves,)),
             pltpu.SemaphoreType.DMA((5,)),
-            pltpu.SemaphoreType.DMA((3,)),
             pltpu.SemaphoreType.DMA((SECTIONS, 2)),
             pltpu.SemaphoreType.DMA((SECTIONS, 2)),
             pltpu.SemaphoreType.DMA,

time: 21.9 us -> 18.9 us (0.86)
  Pallas kernels: 19.3 us -> 17.7 us
  local copies, waits for them, and re-layouts: 2.39 us -> 1 us
    pallas_call x1, Pallas kernels: 19.3 us -> 17.7 us  [body(): pl.pallas_call(functools.partial(kernel, rows, n, samples, variables, cou...]
    unnamed x1, local copies, waits for them, and re-layouts: 2.39 us -> 1 us
where the time goes in v3:
time: 18.9 us; the launch traced here: 18.7 us
  Pallas kernels  17.7 us (94%)
  local copies, waits for them, and re-layouts  1 us (5%)
    pallas_call x1, Pallas kernels, body(): pl.pallas_call(functools.partial(kernel, rows, n, samples, variables, cou...  17.7 us
    unnamed x1, local copies, waits for them, and re-layouts  1 us

profile of v3, /device:TPU:24, one launch (start us, length us, event | category | flops | bytes accessed | tf_op | source)
XLA Modules:
  0.0 18.7 jit_solution(9859274725103362866)
XLA Ops:
  0.0 17.7 %shard_map.73 = f32[35,32,256]{2,1,0:T(8,128)S(1)} custom-call(f32[35,32,256]{2,1,0:T(8,128)} %bitcast.6, f32[5,5,32,256]{3,2,1,0:T(8,128)} %bitcast.7, f32[5,1,5]{2,1,0:T(1,128)} %bitcast.9, s32[2,3]{1,0:T(2,128)} %harm_hbm.1, f32[2]{0:T(128)} %delay_hbm.1, f32[5,7,32]{2,1,0:T(8,128)} %bitcast.8, s32[1,32]{1,0:T(1,128)} %pairing_hbm.1), custom_call_target="tpu_custom_call" | custom-call | flops 34406400 | bytes 3112960 | tf_op jit(solution)/shard_map/pallas_call | solution.py:281
  17.7 1.0 %copy.9 = f32[1,7,5,32,256]{4,3,2,1,0:T(8,128)} copy(f32[1,7,5,32,256]{4,3,2,1,0:T(8,128)S(1)} %bitcast.5) | data formatting | bytes 2293760

commit v4 on v3

--- a/solution.py
+++ b/solution.py
@@ -246,16 +246,22 @@
         def _(k):
             tile(s, k, src, dst)
 
-        finish_down(s, src)
-        tile(s, 0, src, dst)
-        if s < SECTIONS - 1:
-            pack_down(s + 1, dst)
-            start_down(s + 1)
-        finish_up(s, src)
-        tile(s, tiles - 1, src, dst)
-        if s < SECTIONS - 1:
-            pack_up(s + 1, dst)
-            start_up(s + 1)
+        @pl.loop(0, 2)
+        def _(i):
+            side = lax.rem(me + 1 + i, 2)
+            pl.when(side == 0)(lambda: finish_down(s, src))
+            pl.when(side == 1)(lambda: finish_up(s, src))
+            tile(s, side * (tiles - 1), src, dst)
+            if s < SECTIONS - 1:
+                @pl.when(side == 0)
+                def _():
+                    pack_down(s + 1, dst)
+                    start_down(s + 1)
+
+                @pl.when(side == 1)
+                def _():
+                    pack_up(s + 1, dst)
+                    start_up(s + 1)
 
     section(0, q0, qa)
     section(1, qa, qb)

time: 18.9 us -> 19.1 us (1.011)
  the two profiles are of different devices: /device:TPU:24 before, /device:TPU:28 now
where the time goes in v4:
time: 19.1 us; the launch traced here: 18.9 us
  Pallas kernels  17.9 us (94%)
  local copies, waits for them, and re-layouts  1 us (5%)
    pallas_call x1, Pallas kernels, body(): pl.pallas_call(functools.partial(kernel, rows, n, samples, variables, cou...  17.9 us
    unnamed x1, local copies, waits for them, and re-layouts  1 us

profile of v4, /device:TPU:28, one launch (start us, length us, event | category | flops | bytes accessed | tf_op | source)
XLA Modules:
  0.0 18.9 jit_solution(17979813725398920132)
XLA Ops:
  0.0 17.9 %shard_map.73 = f32[35,32,256]{2,1,0:T(8,128)S(1)} custom-call(f32[35,32,256]{2,1,0:T(8,128)} %bitcast.6, f32[5,5,32,256]{3,2,1,0:T(8,128)} %bitcast.7, f32[5,1,5]{2,1,0:T(1,128)} %bitcast.9, s32[2,3]{1,0:T(2,128)} %harm_hbm.1, f32[2]{0:T(128)} %delay_hbm.1, f32[5,7,32]{2,1,0:T(8,128)} %bitcast.8, s32[1,32]{1,0:T(1,128)} %pairing_hbm.1), custom_call_target="tpu_custom_call" | custom-call | flops 34406400 | bytes 3112960 | tf_op jit(solution)/shard_map/pallas_call | solution.py:287
  17.9 1.0 %copy.9 = f32[1,7,5,32,256]{4,3,2,1,0:T(8,128)} copy(f32[1,7,5,32,256]{4,3,2,1,0:T(8,128)S(1)} %bitcast.5) | data formatting | bytes 2293760
